TPU v7x, 512 devices: a whole 4x4x16 slice. The times are simulated.
512 devices in a mesh: grp: 16 (over z), pair: 32 (over x, y, core).
Axes of the slice: x: 4, y: 4, z: 16, core: 2. Of those that a mesh axis runs over, the one named last changes fastest.
Arguments:
- orbital_ints: bfloat16 [1024, 256, 256], P(('grp', 'pair')), may hold values from -1.5 to 1.5
- pair_fock: float32 [16384, 2], P(('grp', 'pair')), may hold values from -2 to -0.2
- pair_orbitals: int32 [16384, 2], P(('grp', 'pair')), may hold values from 0 to 1023, as said below
- rank_bucket: int32 [16384], P(('grp', 'pair')), may hold values from 1 to 3
- pno_coeffs: bfloat16 [16384, 256, 96], P(('grp', 'pair')), may hold values from -0.375 to 0.375
- pno_energy: float32 [16384, 96], P(('grp', 'pair')), may hold values from 0.2 to 4
- amplitudes: bfloat16 [16384, 96, 96], P(('grp', 'pair')), may hold values from -1.796875 to 1.796875
- neighbors: int32 [16384, 2], P(('grp', 'pair')), may hold values from 0 to 16383, as said below
- intersections: bfloat16 [16384, 2, 96, 96], P(('grp', 'pair')), may hold values from -1.1953125 to 1.1953125
- coupling_fock: float32 [16384, 2], P(('grp', 'pair')), may hold values from -4 to 4
Outputs:
- residual: float32 [16384, 96, 96], P(('grp', 'pair'))
Inputs may be any that keep to these rules, and one draw needn't show every extreme that they name: `pair_orbitals`: pair p's first orbital is held by the device that owns pair p. Its second orbital is held by the device with the same pair index in some grp group. Among the pairs of one device, at most 4 have their second orbital in any one group, and exactly 4 in some group. `neighbors`: neighbor pairs belong to the same grp group as the pair. Among the 64 references of the rows of one device, at most 4 point to pairs of any one device, and exactly 4 to some device.
All inputs are finite; a program needn't handle non-finite values.
Results may differ from a plain program's by a relative error of at most 0.0055.
Values may be sent and summed in bfloat16 or wider, within the bound.
A program may use at most 128 MiB of HBM per device.

v0:
```python
import jax
import jax.numpy as jnp
from jax import lax
from jax.sharding import PartitionSpec as P


def slot_table(targets, peer_count, capacity):
    onehot_peer = (targets[:, None] == jnp.arange(peer_count, dtype=jnp.int32)[None, :]).astype(
        jnp.int32
    )
    running = jnp.cumsum(onehot_peer, axis=0) - 1
    position = jnp.sum(running * onehot_peer, axis=1)
    slot_index = targets * capacity + position
    return slot_index[None, :] == jnp.arange(peer_count * capacity, dtype=jnp.int32)[:, None]


def local(
    orbital_ints,
    pair_fock,
    pair_orbitals,
    rank_bucket,
    pno_coeffs,
    pno_energy,
    amplitudes,
    neighbors,
    intersections,
    coupling_fock,
):
    grp_count = lax.axis_size("grp")
    pair_count = lax.axis_size("pair")
    orbital_count = orbital_ints.shape[0]
    aux_width = orbital_ints.shape[1]
    pair_local = pno_coeffs.shape[0]
    virtual_width = pno_coeffs.shape[1]
    rank_width = pno_coeffs.shape[2]
    neighbor_count = neighbors.shape[1]
    device_index = lax.axis_index("grp") * pair_count + lax.axis_index("pair")
    positions = jnp.arange(rank_width, dtype=jnp.int32)
    live_rows = positions[None, :] < (rank_bucket * (rank_width // 3))[:, None]
    live_block = live_rows[:, :, None] & live_rows[:, None, :]
    first_local = pair_orbitals[:, 0] - device_index * orbital_count
    second_orbital = pair_orbitals[:, 1]
    first_blocks = jnp.take(orbital_ints, first_local, axis=0)
    first_transformed = jnp.einsum(
        "pqv,pvr->pqr", first_blocks, pno_coeffs, preferred_element_type=jnp.float32
    ).astype(jnp.bfloat16)
    owner_group = second_orbital // (pair_count * orbital_count)
    owner_local = second_orbital % orbital_count
    capacity = max(2, 2 * pair_local // grp_count)
    placed = slot_table(owner_group, grp_count, capacity)
    placed_half = placed.astype(jnp.bfloat16)
    outgoing = jnp.dot(
        placed_half,
        pno_coeffs.reshape(pair_local, virtual_width * rank_width),
        preferred_element_type=jnp.float32,
    ).astype(jnp.bfloat16)
    outgoing = outgoing.reshape(grp_count, capacity, virtual_width, rank_width)
    wanted = jnp.sum(jnp.where(placed, owner_local[None, :], 0), axis=1).reshape(
        grp_count, capacity
    )
    coeffs_in = lax.all_to_all(outgoing, "grp", split_axis=0, concat_axis=0, tiled=True)
    wanted_in = lax.all_to_all(wanted, "grp", split_axis=0, concat_axis=0, tiled=True)
    blocks_in = jnp.take(orbital_ints, wanted_in, axis=0)
    product = jnp.einsum(
        "gkqv,gkvr->gkqr", blocks_in, coeffs_in, preferred_element_type=jnp.float32
    ).astype(jnp.bfloat16)
    returned = lax.all_to_all(product, "grp", split_axis=0, concat_axis=0, tiled=True)
    second_transformed = jnp.dot(
        placed_half.T,
        returned.reshape(grp_count * capacity, aux_width * rank_width),
        preferred_element_type=jnp.float32,
    ).astype(jnp.bfloat16)
    second_transformed = second_transformed.reshape(pair_local, aux_width, rank_width)
    masked_amplitudes = jnp.where(live_block, amplitudes, jnp.zeros_like(amplitudes))
    references = neighbors.reshape(-1)
    target_column = references // pair_local % pair_count
    target_local = references % pair_local
    capacity_near = max(2, 2 * pair_local * neighbor_count // pair_count)
    placed_near = slot_table(target_column, pair_count, capacity_near)
    requested = jnp.sum(jnp.where(placed_near, target_local[None, :], 0), axis=1).reshape(
        pair_count, capacity_near
    )
    found_amps = jnp.take(
        masked_amplitudes,
        lax.all_to_all(requested, "pair", split_axis=0, concat_axis=0, tiled=True),
        axis=0,
    )
    arrived = lax.all_to_all(found_amps, "pair", split_axis=0, concat_axis=0, tiled=True)
    exchange_integrals = jnp.einsum(
        "pqa,pqb->pab", first_transformed, second_transformed, preferred_element_type=jnp.float32
    )
    energy_gap = (
        pno_energy[:, :, None]
        + pno_energy[:, None, :]
        - (pair_fock[:, 0] + pair_fock[:, 1])[:, None, None]
    )
    diagonal_term = energy_gap * amplitudes.astype(jnp.float32)
    neighbor_amps = jnp.dot(
        placed_near.T.astype(jnp.bfloat16),
        arrived.reshape(pair_count * capacity_near, rank_width * rank_width),
        preferred_element_type=jnp.float32,
    ).astype(jnp.bfloat16)
    neighbor_amps = neighbor_amps.reshape(pair_local, neighbor_count, rank_width, rank_width)
    half_coupled = jnp.einsum(
        "pnac,pncd->pnad", intersections, neighbor_amps, preferred_element_type=jnp.float32
    ).astype(jnp.bfloat16)
    coupled = jnp.einsum(
        "pnad,pnbd->pnab", half_coupled, intersections, preferred_element_type=jnp.float32
    )
    coupling = jnp.sum(coupling_fock[:, :, None, None] * coupled, axis=1)
    total = exchange_integrals + diagonal_term - coupling
    return jnp.where(live_block, total, jnp.zeros_like(total))


def solution(mesh):
    return jax.shard_map(
        local,
        mesh=mesh,
        in_specs=(
            P(("grp", "pair"), None, None),
            P(("grp", "pair"), None),
            P(("grp", "pair"), None),
            P(("grp", "pair")),
            P(("grp", "pair"), None, None),
            P(("grp", "pair"), None),
            P(("grp", "pair"), None, None),
            P(("grp", "pair"), None),
            P(("grp", "pair"), None, None, None),
            P(("grp", "pair"), None),
        ),
        out_specs=P(("grp", "pair"), None, None),
        check_vma=False,
    )
```

profile of v0, /device:TPU:8, one launch (start us, length us, event | category | flops | bytes accessed | tf_op | source)
XLA Modules:
  0.0 424.2 jit_solution(17165976694150763391)
XLA Ops:
  2.2 9.3 %all-to-all-start.3 = ((s32[32,1,4]{2,1,0:T(1,128)}), s32[32,1,4]{2,1,0:T(1,128)S(1)}, u32[]{:S(2)}, u32[]{:S(2)}) async-start(s32[32,1,4]{2,1,0:T(1,128)} %bitcast.9), calls=%async_computation.3 | async-start | bytes 32768 | tf_op jit(solution)/shard_map/all_to_all | solution.py:85
  13.3 3.9 copy.60
  17.2 4.2 reshape.306
  22.1 13.4 %all-to-all-start = ((s32[16,1,4]{2,1,0:T(1,128)}), s32[16,1,4]{2,1,0:T(1,128)S(1)}, u32[]{:S(2)}, u32[]{:S(2)}) async-start(s32[16,1,4]{2,1,0:T(1,128)} %bitcast.4), calls=%async_computation | async-start | bytes 16384 | tf_op jit(solution)/shard_map/all_to_all | solution.py:62
  35.6 2.6 convolution_convert_fusion
  38.2 6.7 %reshape.307 = bf16[16,4,256,96]{3,2,1,0:T(8,128)(2,1)} reshape(bf16[64,24576]{1,0:T(8,128)(2,1)} %convolution_convert_fusion) | data formatting | bytes 6291456 | tf_op jit(solution)/shard_map/reshape | solution.py:57
  44.9 6.1 %copy.61 = bf16[16,4,256,96]{2,3,1,0:T(8,128)(2,1)} copy(bf16[16,4,256,96]{3,2,1,0:T(8,128)(2,1)} %reshape.307) | data formatting | bytes 6291456 | tf_op jit(solution)/shard_map/reshape | solution.py:57
  51.0 12.2 %all-to-all-start.1 = ((bf16[16,4,256,96]{2,3,1,0:T(8,128)(2,1)}), bf16[16,4,256,96]{2,3,1,0:T(8,128)(2,1)}, u32[]{:S(2)}, u32[]{:S(2)}) async-start(bf16[16,4,256,96]{2,3,1,0:T(8,128)(2,1)} %copy.61), calls=%async_computation.1 | async-start | bytes 6291456 | tf_op jit(solution)/shard_map/all_to_all | solution.py:61
  66.9 3.9 broadcast_select_fusion
  70.8 131.7 %all-to-all-done.1 = bf16[16,4,256,96]{2,3,1,0:T(8,128)(2,1)} async-done(((bf16[16,4,256,96]{2,3,1,0:T(8,128)(2,1)}), bf16[16,4,256,96]{2,3,1,0:T(8,128)(2,1)}, u32[]{:S(2)}, u32[]{:S(2)}) %all-to-all-start.1) | async-done | bytes 3145760 | tf_op jit(solution)/shard_map/all_to_all | solution.py:61
  202.4 7.4 %all-to-all-start.4 = ((bf16[32,4,96,96]{3,2,1,0:T(8,128)(2,1)}), bf16[32,4,96,96]{3,2,1,0:T(8,128)(2,1)}, u32[]{:S(2)}, u32[]{:S(2)}) async-start(bf16[32,4,96,96]{3,2,1,0:T(8,128)(2,1)} %broadcast_select_fusion), calls=%async_computation.4 | async-start | bytes 6291456 | tf_op jit(solution)/shard_map/all_to_all | solution.py:88
  210.3 5.3 %gather_fusion.1 = bf16[64,256,256]{2,1,0:T(8,128)(2,1)} fusion(bf16[2,256,256]{2,1,0:T(8,128)(2,1)S(1)} %copy-done.1, s32[1024]{0:T(1024)S(1)} %pad_clamp_fusion.1), kind=kCustom, calls=%fused_computation.1 | custom fusion | bytes 16777472 | tf_op jit(solution)/shard_map/jit(_take)/gather | solution.py:63
  215.6 8.8 %fusion.7 = bf16[16,4,256,96]{2,3,1,0:T(8,128)(2,1)} fusion(bf16[16,4,256,96]{2,3,1,0:T(8,128)(2,1)} %all-to-all-done.1, bf16[16,4,256,256]{3,2,1,0:T(8,128)(2,1)} %bitcast.56, pred[16,4]{1,0:T(8,128)(4,1)S(1)} %copy.57), kind=kOutput, calls=%fused_computation.15 | convolution fusion | flops 811073536 | bytes 14680128 | tf_op jit(solution)/shard_map/gkqv,gkvr->gkqr/dot_general | solution.py:64
  224.4 25.1 %all-to-all-done.4 = bf16[32,4,96,96]{3,2,1,0:T(8,128)(2,1)} async-done(((bf16[32,4,96,96]{3,2,1,0:T(8,128)(2,1)}), bf16[32,4,96,96]{3,2,1,0:T(8,128)(2,1)}, u32[]{:S(2)}, u32[]{:S(2)}) %all-to-all-start.4) | async-done | bytes 2359328 | tf_op jit(solution)/shard_map/all_to_all | solution.py:88
  249.4 8.4 %all-to-all-start.2 = ((bf16[16,4,256,96]{2,3,1,0:T(8,128)(2,1)}), bf16[16,4,256,96]{2,3,1,0:T(8,128)(2,1)}, u32[]{:S(2)}, u32[]{:S(2)}) async-start(bf16[16,4,256,96]{2,3,1,0:T(8,128)(2,1)} %fusion.7), calls=%async_computation.2 | async-start | bytes 6291456 | tf_op jit(solution)/shard_map/all_to_all | solution.py:67
  258.0 2.8 gather_fusion
  260.8 6.7 %reshape.311 = bf16[128,9216]{1,0:T(8,128)(2,1)} reshape(bf16[32,4,96,96]{3,2,1,0:T(8,128)(2,1)} %all-to-all-done.4) | data formatting | bytes 4718592 | tf_op jit(solution)/shard_map/reshape | solution.py:100
  267.5 3.2 convolution_convert_fusion.2
  273.3 3.3 multiply_reduce_fusion
  276.6 120.7 %all-to-all-done.2 = bf16[16,4,256,96]{2,3,1,0:T(8,128)(2,1)} async-done(((bf16[16,4,256,96]{2,3,1,0:T(8,128)(2,1)}), bf16[16,4,256,96]{2,3,1,0:T(8,128)(2,1)}, u32[]{:S(2)}, u32[]{:S(2)}) %all-to-all-start.2) | async-done | bytes 3145760 | tf_op jit(solution)/shard_map/all_to_all | solution.py:67
  397.3 6.0 %copy.62 = bf16[16,4,256,96]{3,2,1,0:T(8,128)(2,1)} copy(bf16[16,4,256,96]{2,3,1,0:T(8,128)(2,1)} %all-to-all-done.2) | data formatting | bytes 6291456 | tf_op jit(solution)/shard_map/all_to_all | solution.py:67
  403.3 8.1 %reshape.308 = bf16[64,24576]{1,0:T(8,128)(2,1)} reshape(bf16[16,4,256,96]{3,2,1,0:T(8,128)(2,1)} %copy.62) | data formatting | bytes 6291456 | tf_op jit(solution)/shard_map/reshape | solution.py:70
  414.0 3.1 reshape.309
  417.1 7.1 %and_select_fusion = f32[32,96,96]{2,1,0:T(8,128)} fusion(f32[32,96,96]{2,1,0:T(8,128)} %multiply_reduce_fusion, bf16[32,96,96]{2,1,0:T(8,128)(2,1)} %param.16, bf16[32,256,96]{2,1,0:T(8,128)(2,1)} %reshape.309, bf16[32,256,96]{1,2,0:T(8,128)(2,1)} %param.14, bf16[32,256,256]{2,1,0:T(8,128)(2,1)} %gather_fusion, pred[32]{0:T(512)(128)(4,1)S(1)} %get-tuple-element.5, ...), kind=kOutput, calls=%fused_computation.17 | convolution fusion | flops 558891008 | bytes 10304672 | tf_op jit(solution)/shard_map/pqa,pqb->pab/dot_general | solution.py:89
  (58 shorter events, 14.0 us)
Async XLA Ops:
  0.0 273.3 %copy-start = (bf16[32,2,96,96]{3,2,1,0:T(8,128)(2,1)S(1)}, bf16[32,2,96,96]{3,2,1,0:T(8,128)(2,1)}, u32[]{:S(2)}) copy-start(bf16[32,2,96,96]{3,2,1,0:T(8,128)(2,1)} %param.18) | copy-start | bytes 3538948
  2.2 19.9 %all-to-all-start.3 = ((s32[32,1,4]{2,1,0:T(1,128)}), s32[32,1,4]{2,1,0:T(1,128)S(1)}, u32[]{:S(2)}, u32[]{:S(2)}) async-start(s32[32,1,4]{2,1,0:T(1,128)} %bitcast.9), calls=%async_computation.3 | async-start | bytes 32768 | tf_op jit(solution)/shard_map/all_to_all | solution.py:85
  22.1 28.9 %all-to-all-start = ((s32[16,1,4]{2,1,0:T(1,128)}), s32[16,1,4]{2,1,0:T(1,128)S(1)}, u32[]{:S(2)}, u32[]{:S(2)}) async-start(s32[16,1,4]{2,1,0:T(1,128)} %bitcast.4), calls=%async_computation | async-start | bytes 16384 | tf_op jit(solution)/shard_map/all_to_all | solution.py:62
  51.0 12.2 %copy-start.7 = (s32[32]{0:T(128)S(1)}, s32[32]{0:T(128)}, u32[]{:S(2)}) copy-start(s32[32]{0:T(128)} %param.13) | copy-start | bytes 388
  51.0 12.3 %copy-start.2 = (bf16[32,96,96]{2,1,0:T(8,128)(2,1)S(1)}, bf16[32,96,96]{2,1,0:T(8,128)(2,1)}, u32[]{:S(2)}) copy-start(bf16[32,96,96]{2,1,0:T(8,128)(2,1)} %param.16) | copy-start | bytes 1769476
  51.0 151.4 %all-to-all-start.1 = ((bf16[16,4,256,96]{2,3,1,0:T(8,128)(2,1)}), bf16[16,4,256,96]{2,3,1,0:T(8,128)(2,1)}, u32[]{:S(2)}, u32[]{:S(2)}) async-start(bf16[16,4,256,96]{2,3,1,0:T(8,128)(2,1)} %copy.61), calls=%async_computation.1 | async-start | bytes 6291456 | tf_op jit(solution)/shard_map/all_to_all | solution.py:61
  70.8 139.5 %copy-start.1 = (bf16[2,256,256]{2,1,0:T(8,128)(2,1)S(1)}, bf16[2,256,256]{2,1,0:T(8,128)(2,1)}, u32[]{:S(2)}) copy-start(bf16[2,256,256]{2,1,0:T(8,128)(2,1)} %param.10) | copy-start | bytes 786436
  202.4 47.0 %all-to-all-start.4 = ((bf16[32,4,96,96]{3,2,1,0:T(8,128)(2,1)}), bf16[32,4,96,96]{3,2,1,0:T(8,128)(2,1)}, u32[]{:S(2)}, u32[]{:S(2)}) async-start(bf16[32,4,96,96]{3,2,1,0:T(8,128)(2,1)} %broadcast_select_fusion), calls=%async_computation.4 | async-start | bytes 6291456 | tf_op jit(solution)/shard_map/all_to_all | solution.py:88
  224.4 33.5 %copy-start.3 = (f32[32,2]{0,1:T(2,128)S(1)}, f32[32,2]{0,1:T(2,128)}, u32[]{:S(2)}) copy-start(f32[32,2]{0,1:T(2,128)} %param.19) | copy-start | bytes 772
  224.4 33.6 %copy-start.4 = (s32[32,2]{0,1:T(2,128)S(1)}, s32[32,2]{0,1:T(2,128)}, u32[]{:S(2)}) copy-start(s32[32,2]{0,1:T(2,128)} %param.12) | copy-start | bytes 772
  249.4 147.9 %all-to-all-start.2 = ((bf16[16,4,256,96]{2,3,1,0:T(8,128)(2,1)}), bf16[16,4,256,96]{2,3,1,0:T(8,128)(2,1)}, u32[]{:S(2)}, u32[]{:S(2)}) async-start(bf16[16,4,256,96]{2,3,1,0:T(8,128)(2,1)} %fusion.7), calls=%async_computation.2 | async-start | bytes 6291456 | tf_op jit(solution)/shard_map/all_to_all | solution.py:67
  258.0 2.8 copy-start.6
  414.0 3.1 copy-start.5
where the time goes:
time: 425 us; the launch traced here: 424 us
  waiting for transfers between devices  277 us (65%)
  local copies, waits for them, and re-layouts  61.3 us (14%)
  starting transfers between devices  50.8 us (12%)
  matrix products  27.5 us (6%)
  other arithmetic  6.86 us (2%)
    all_to_all x1, waiting for transfers between devices, local(): lax.all_to_all(outgoing, 'grp', split_axis=0, concat_axis=0, tiled=True)  132 us
    all_to_all x1, waiting for transfers between devices, local(): lax.all_to_all(product, 'grp', split_axis=0, concat_axis=0, tiled=True)  121 us
    all_to_all x1, waiting for transfers between devices, local(): lax.all_to_all(found_amps, 'pair', split_axis=0, concat_axis=0, tiled=True)  25.1 us
    all_to_all x1, starting transfers between devices, local(): lax.all_to_all(wanted, 'grp', split_axis=0, concat_axis=0, tiled=True)  13.4 us
    reshape x2, local copies, waits for them, and re-layouts, local(): outgoing = outgoing.reshape(grp_count, capacity, virtual_width, rank_width)  12.8 us
    all_to_all x1, starting transfers between devices, local(): lax.all_to_all(outgoing, 'grp', split_axis=0, concat_axis=0, tiled=True)  12.2 us
    all_to_all x1, starting transfers between devices, local(): lax.all_to_all(requested, 'pair', split_axis=0, concat_axis=0, tiled=True)  9.31 us
    dot_general x1, matrix products, local(): jnp.einsum('gkqv,gkvr->gkqr', blocks_in, coeffs_in, preferred_element_typ...  8.76 us
  transfers between devices with their start and end apart: 5, of which 3 were waited for; matrix products, arithmetic and copies ran while one was open for 16% of the time, Pallas kernels for 0%

commit v1 on v0

v1 whole, which is shorter than its diff:
```python
import functools

import jax
import jax.numpy as jnp
from jax import lax
from jax.experimental import pallas as pl
from jax.experimental.pallas import tpu as pltpu
from jax.sharding import PartitionSpec as P

MESH = pl.DeviceIdType.MESH
BF16 = jnp.bfloat16
F32 = jnp.float32
NT = (((1,), (1,)), ((), ()))
NN = (((1,), (0,)), ((), ()))

GROUPS = 16
PEERS = 32
PAIRS = 32
R = 96
AUX = 256
SLOTS = 4
CHUNKS = 4
HALF = GROUPS // 2
ROWS = 2 * AUX // CHUNKS
STRIDE = 13
LANES = 128


def dot(a, b, dims):
    return lax.dot_general(a, b, dims, preferred_element_type=F32)


def shifted(device, k, sign):
    core, y, x = device % 2, device // 2 % 4, device // 8
    dc, dy, dx = k % 2, k // 2 % 4, k // 8
    return ((x + sign * dx + 4) % 4 * 4 + (y + sign * dy + 4) % 4) * 2 + (core + dc) % 2


def iota(shape, axis):
    return lax.broadcasted_iota(jnp.int32, shape, axis)


def as_column(row):
    n = row.shape[1]
    return jnp.sum(jnp.where(iota((n, n), 0) == iota((n, n), 1), row, 0), axis=1, keepdims=True)


def as_lanes(column):
    n = column.shape[0]
    return jnp.sum(jnp.where(iota((n, LANES), 0) == iota((n, LANES), 1), column, 0), axis=0, keepdims=True)


def scattered(slot, value):
    return jnp.sum(jnp.where(slot == iota((slot.shape[0], LANES), 1), value, 0), axis=0, keepdims=True)


def kernel(
    orb_hbm, coeffs_hbm, amps_hbm, inter_hbm, energy, orbitals, nearby, rank, fock, weight,
    out, orbs, coeffs, amps, masked, inter, first, exchange, coupled, outbox, inbox, asked, table,
    table_s, asked_s, local_sem, ring_out, ring_in, ask_out, ask_in, amp_out, amp_in,
):
    grp = lax.axis_index("grp")
    me = lax.axis_index("pair")
    right = lax.rem(grp + 1, GROUPS)
    left = lax.rem(grp + GROUPS - 1, GROUPS)

    own_orbs = pltpu.make_async_copy(orb_hbm, orbs.at[0], local_sem.at[0])
    own_coeffs = pltpu.make_async_copy(coeffs_hbm, coeffs, local_sem.at[1])
    own_amps = pltpu.make_async_copy(amps_hbm, amps, local_sem.at[2])
    own_inter = pltpu.make_async_copy(inter_hbm, inter, local_sem.at[3])
    own_orbs.start()

    barrier = pltpu.get_barrier_semaphore()
    for target in (right, left):
        pl.semaphore_signal(barrier, inc=1, device_id=(target, me), device_id_type=MESH)

    @pl.loop(1, PEERS)
    def _(k):
        pl.semaphore_signal(barrier, inc=1, device_id=(grp, shifted(me, k, 1)), device_id_type=MESH)

    own_amps.start()
    own_coeffs.start()
    own_inter.start()
    own_orbs.wait()
    pl.semaphore_wait(barrier, PEERS + 1)

    def ring(d, s, c):
        chunk = c if d == 0 else CHUNKS - 1 - c
        rows = pl.ds(chunk * ROWS, ROWS)
        here = (GROUPS - (s - 1)) % GROUPS if d == 0 else s - 1
        there = GROUPS - s if d == 0 else s
        return pltpu.make_async_remote_copy(
            orbs.at[here, rows], orbs.at[there, rows], ring_out.at[d, s - 1, c], ring_in.at[d, s - 1, c],
            device_id=(right if d == 0 else left, me), device_id_type=MESH,
        )

    def ask(k):
        return pltpu.make_async_remote_copy(
            table.at[pl.ds(0, 1)], asked.at[pl.ds(k, 1)], ask_out.at[k], ask_in.at[k],
            device_id=(grp, shifted(me, k, 1)), device_id_type=MESH,
        )

    def answer(k):
        return pltpu.make_async_remote_copy(
            outbox.at[k], inbox.at[k], amp_out.at[k], amp_in.at[k],
            device_id=(grp, shifted(me, k, -1)), device_id_type=MESH,
        )

    @pl.loop(0, CHUNKS)
    def _(c):
        ring(0, 1, c).start()
        ring(1, 1, c).start()

    above = iota((PAIRS, PAIRS), 1) < iota((PAIRS, PAIRS), 0)

    def same(column, row):
        return column == row

    def count(hits):
        return jnp.sum(jnp.where(hits, 1, 0), axis=1, keepdims=True)

    def within(place):
        return jnp.minimum(place, SLOTS - 1)

    column_of = (nearby[...] >> 5) & (PEERS - 1)
    core, y, x = me % 2, me // 2 % 4, me // 8
    distance = (((column_of >> 3) - x) & 3) * 8 + ((((column_of >> 1) & 3) - y) & 3) * 2 + ((column_of - core) & 1)
    at = nearby[...] & (PAIRS - 1)
    rows = [distance[0:1], distance[1:2]]
    columns = [as_column(r) for r in rows]
    wanted = [as_column(at[0:1]), as_column(at[1:2])]
    place = [
        columns[0] * SLOTS + within(count(same(columns[0], rows[0]) & above)),
        columns[1] * SLOTS + within(count(same(columns[1], rows[0])) + count(same(columns[1], rows[1]) & above)),
    ]
    pair = iota((PAIRS, 1), 0)
    table[0:1] = (scattered(place[0], wanted[0]) + scattered(place[1], wanted[1])) & (PAIRS - 1)

    @pl.loop(1, PEERS)
    def _(k):
        ask((k * STRIDE) % PEERS).start()

    table[1:2] = (scattered(place[0], 2 * pair) + scattered(place[1], 2 * pair + 1)) & (2 * PAIRS - 1)
    table[2:3] = as_lanes(place[0])
    table[3:4] = as_lanes(place[1])
    second = orbitals[1:2]
    home = ((second >> 6) - grp) & (GROUPS - 1)
    home_column = as_column(home)
    home_place = home_column * SLOTS + within(count(same(home_column, home) & above))
    table[4:5] = scattered(home_place, pair) & (PAIRS - 1)
    table[5:6] = scattered(home_place, as_column(second & 1))
    table[6:7] = as_lanes(home_place)
    table[7:8] = as_lanes(as_column(orbitals[0:1] & 1))
    to_scalar = pltpu.make_async_copy(table, table_s, local_sem.at[4])
    to_scalar.start()
    own_amps.wait()

    def live(p):
        top = rank[p] * (R // 3)
        return (iota((R, R), 0) < top) & (iota((R, R), 1) < top)

    def mask_pair(p, _):
        mine = amps[p].astype(F32)
        masked[p] = jnp.where(live(p), mine, 0.0).astype(BF16)
        return 0

    lax.fori_loop(0, PAIRS, mask_pair, 0, unroll=4)
    to_scalar.wait()
    own_coeffs.wait()

    def first_pair(p, _):
        half = table_s[7, p]
        block = jnp.where(half == 1, orbs[0, AUX:], orbs[0, :AUX])
        first[p] = dot(coeffs[p], block, NT).astype(BF16)
        return 0

    lax.fori_loop(0, PAIRS, first_pair, 0, unroll=4)

    @pl.loop(1, PEERS)
    def _(k):
        ask(k).wait_recv()

    asked_in = pltpu.make_async_copy(asked, asked_s, local_sem.at[5])
    asked_in.start()
    asked_in.wait()

    @pl.loop(1, PEERS)
    def _(i):
        k = (i * STRIDE) % PEERS
        blocks = [masked[asked_s[k, SLOTS * k + j]] for j in range(SLOTS)]
        for j in range(3):
            outbox[k, j] = jnp.concatenate([blocks[j], blocks[3][:, 32 * j : 32 * j + 32]], axis=1)
        answer(k).start()

    own_inter.wait()

    def exchange_slot(kz, j):
        slot = kz * SLOTS + j
        p, half = table_s[4, slot], table_s[5, slot]
        block = jnp.where(half == 1, orbs[kz, AUX:], orbs[kz, :AUX])
        moved = dot(coeffs[p], block, NT).astype(BF16)
        exchange[slot] = dot(first[p], moved, NT)

    def couple(slot, block):
        t = inter[table_s[1, slot]]
        coupled[slot] = dot(dot(t, block, NN).astype(BF16), t, NT)

    def couple_own():
        for j in range(SLOTS):
            couple(j, masked[table_s[0, j]])

    def couple_peer(k):
        answer(k).wait_recv()
        parts = [inbox[k, j] for j in range(3)]
        for j in range(3):
            couple(SLOTS * k + j, parts[j][:, :R])
        couple(SLOTS * k + 3, jnp.concatenate([part[:, R:] for part in parts], axis=1))

    def diagonal(p):
        across = energy[pl.ds(p, 1), :]
        down = jnp.sum(jnp.where(iota((R, R), 0) == iota((R, R), 1), across, 0.0), axis=1, keepdims=True)
        out[p] = (down + across - (fock[0, p] + fock[1, p])) * amps[p].astype(F32)

    def forward(s, c):
        for d in (0, 1):
            ring(d, s - 1, c).wait_recv()
            ring(d, s, c).start()

    def exchange_some(s, c):
        kz = jnp.where(c < 2, s, (GROUPS - s) % GROUPS)
        for j in range(2):
            exchange_slot(kz, c % 2 * 2 + j)

    @pl.loop(0, CHUNKS)
    def _(c):
        forward(2, c)
        exchange_some(0, c)

        @pl.loop(0, PAIRS // CHUNKS)
        def _(p):
            diagonal(c * (PAIRS // CHUNKS) + p)

    couple_own()
    per_unit = 1
    begin = 3

    @pl.loop(begin, HALF)
    def _(s):
        @pl.loop(0, CHUNKS)
        def _(c):
            forward(s, c)
            exchange_some(s - 2, c)
            couple_peer((((s - begin) * CHUNKS + c + 1) * STRIDE) % PEERS)

    done = 1 + (HALF - begin) * CHUNKS

    @pl.loop(0, 2)
    def _(c):
        forward(HALF, c)
        exchange_some(HALF - 2, c)

    @pl.loop(2, CHUNKS)
    def _(c):
        ring(0, HALF - 1, c).wait_recv()
        ring(1, HALF - 1, c).wait_recv()
        exchange_some(HALF - 2, c)

    @pl.loop(0, CHUNKS)
    def _(c):
        exchange_some(HALF - 1, c)

    @pl.loop(done, PEERS)
    def _(i):
        couple_peer((i * STRIDE) % PEERS)

    @pl.loop(0, 2)
    def _(c):
        ring(0, HALF, c).wait_recv()
        ring(1, HALF, c).wait_recv()

    for j in range(SLOTS):
        exchange_slot(HALF, j)

    def finish(p, _):
        near = weight[0, p] * coupled[table_s[2, p]] + weight[1, p] * coupled[table_s[3, p]]
        out[p] = jnp.where(live(p), out[p] + exchange[table_s[6, p]] - near, 0.0)
        return 0

    lax.fori_loop(0, PAIRS, finish, 0, unroll=4)

    @pl.loop(1, PEERS)
    def _(k):
        ask(k).wait_send()
        answer(k).wait_send()

    @pl.loop(1, HALF)
    def _(s):
        @pl.loop(0, CHUNKS)
        def _(c):
            ring(0, s, c).wait_send()
            ring(1, s, c).wait_send()

    @pl.loop(0, 2)
    def _(c):
        ring(0, HALF, c).wait_send()
        ring(1, HALF, c).wait_send()


def local(
    orbital_ints, pair_fock, pair_orbitals, rank_bucket, pno_coeffs, pno_energy, amplitudes, neighbors, intersections, coupling_fock
):
    far = pl.BlockSpec(memory_space=pltpu.HBM)
    vector = pl.BlockSpec(memory_space=pltpu.VMEM)
    scalar = pl.BlockSpec(memory_space=pltpu.SMEM)
    dma = pltpu.SemaphoreType.DMA
    return pl.pallas_call(
        kernel,
        out_shape=jax.ShapeDtypeStruct((PAIRS, R, R), F32),
        in_specs=[far, far, far, far, vector, vector, vector, scalar, scalar, scalar],
        out_specs=vector,
        scratch_shapes=[
            pltpu.VMEM((GROUPS, 2 * AUX, AUX), BF16),
            pltpu.VMEM((PAIRS, R, AUX), BF16),
            pltpu.VMEM((PAIRS, R, R), BF16),
            pltpu.VMEM((PAIRS, R, R), BF16),
            pltpu.VMEM((2 * PAIRS, R, R), BF16),
            pltpu.VMEM((PAIRS, R, AUX), BF16),
            pltpu.VMEM((GROUPS * SLOTS, R, R), F32),
            pltpu.VMEM((PEERS * SLOTS, R, R), F32),
            pltpu.VMEM((PEERS, 3, R, LANES), BF16),
            pltpu.VMEM((PEERS, 3, R, LANES), BF16),
            pltpu.VMEM((PEERS, LANES), jnp.int32),
            pltpu.VMEM((8, LANES), jnp.int32),
            pltpu.SMEM((8, LANES), jnp.int32),
            pltpu.SMEM((PEERS, LANES), jnp.int32),
            dma((6,)),
            dma((2, HALF, CHUNKS)),
            dma((2, HALF, CHUNKS)),
            dma((PEERS,)),
            dma((PEERS,)),
            dma((PEERS,)),
            dma((PEERS,)),
        ],
        compiler_params=pltpu.CompilerParams(
            collective_id=0, has_side_effects=True, vmem_limit_bytes=48 * 2**20
        ),
    )(
        orbital_ints.reshape(2 * AUX, AUX),
        jnp.swapaxes(pno_coeffs, 1, 2),
        amplitudes,
        intersections.reshape(2 * PAIRS, R, R),
        pno_energy,
        pair_orbitals.T,
        neighbors.T,
        rank_bucket,
        pair_fock.T,
        coupling_fock.T,
    )


def solution(mesh):
    rows = P(("grp", "pair"))
    return jax.shard_map(
        local,
        mesh=mesh,
        in_specs=(rows,) * 10,
        out_specs=rows,
        check_vma=False,
    )
```

time: 425 us -> 90.7 us (0.21)
  the two profiles are of different devices: /device:TPU:8 before, /device:TPU:5 now
where the time goes in v1:
time: 90.7 us; the launch traced here: 90.3 us
  Pallas kernels  80.2 us (88%)
  local copies, waits for them, and re-layouts  10.1 us (11%)
    pallas_call x1, Pallas kernels, local(): pl.pallas_call(kernel, out_shape=jax.ShapeDtypeStruct((PAIRS, R, R), F32)...  80.2 us
    unnamed x21, local copies, waits for them, and re-layouts  10.1 us

profile of v1, /device:TPU:5, one launch (start us, length us, event | category | flops | bytes accessed | tf_op | source)
XLA Modules:
  0.0 90.3 jit_solution(4380166627072619651)
XLA Ops:
  0.0 0.0 copy-start
  0.0 1.4 %copy-done = bf16[32,256,96]{1,2,0:T(8,128)(2,1)S(1)} copy-done((bf16[32,256,96]{1,2,0:T(8,128)(2,1)S(1)}, bf16[32,256,96]{1,2,0:T(8,128)(2,1)}, u32[]{:S(2)}) %copy-start) | copy-done | bytes 1572888
  1.4 0.0 copy-start.1
  1.4 1.4 %copy-done.1 = bf16[32,2,96,96]{3,2,1,0:T(8,128)(2,1)S(1)} copy-done((bf16[32,2,96,96]{3,2,1,0:T(8,128)(2,1)S(1)}, bf16[32,2,96,96]{3,2,1,0:T(8,128)(2,1)}, u32[]{:S(2)}) %copy-start.1) | copy-done | bytes 1179672
  2.8 0.0 copy-start.2
  2.8 1.1 %copy-done.2 = bf16[32,96,96]{2,1,0:T(8,128)(2,1)S(1)} copy-done((bf16[32,96,96]{2,1,0:T(8,128)(2,1)S(1)}, bf16[32,96,96]{2,1,0:T(8,128)(2,1)}, u32[]{:S(2)}) %copy-start.2) | copy-done | bytes 589848
  4.0 0.0 copy-start.3
  4.0 0.9 %copy-done.3 = bf16[2,256,256]{2,1,0:T(8,128)(2,1)S(1)} copy-done((bf16[2,256,256]{2,1,0:T(8,128)(2,1)S(1)}, bf16[2,256,256]{2,1,0:T(8,128)(2,1)}, u32[]{:S(2)}) %copy-start.3) | copy-done | bytes 262168
  4.9 0.0 copy-start.4
  4.9 0.7 copy-done.4
  5.6 0.0 copy-start.5
  5.6 0.7 copy-done.5
  6.3 0.0 copy-start.6
  6.3 0.7 copy-done.6
  7.0 0.0 copy-start.7
  7.0 0.7 copy-done.7
  7.7 0.0 copy-start.8
  7.7 0.7 copy-done.8
  8.3 0.0 copy-start.9
  8.3 0.7 copy-done.9
  9.0 80.2 %shard_map.100 = f32[32,96,96]{2,1,0:T(8,128)S(1)} custom-call(bf16[512,256]{1,0:T(8,128)(2,1)S(1)} %bitcast.9, bf16[32,96,256]{2,1,0:T(8,128)(2,1)S(1)} %bitcast.7, bf16[32,96,96]{2,1,0:T(8,128)(2,1)S(1)} %copy-done.2, bf16[64,96,96]{2,1,0:T(8,128)(2,1)S(1)} %bitcast.8, f32[32,96]{1,0:T(8,128)S(1)} %copy-done.4, s32[2,32]{1,0:T(2,128)S(1)} %bitcast.10, ...), custom_call_target="tpu_custom_call" | custom-call | tf_op jit(solution)/shard_map/pallas_call | solution.py:316
  89.2 1.1 %copy.12 = f32[32,96,96]{2,1,0:T(8,128)} copy(f32[32,96,96]{2,1,0:T(8,128)S(1)} %shard_map.100) | data formatting | bytes 2359296
Async XLA Ops:
  0.0 1.4 %copy-start = (bf16[32,256,96]{1,2,0:T(8,128)(2,1)S(1)}, bf16[32,256,96]{1,2,0:T(8,128)(2,1)}, u32[]{:S(2)}) copy-start(bf16[32,256,96]{1,2,0:T(8,128)(2,1)} %param.14) | copy-start | bytes 4718596
  1.4 1.4 %copy-start.1 = (bf16[32,2,96,96]{3,2,1,0:T(8,128)(2,1)S(1)}, bf16[32,2,96,96]{3,2,1,0:T(8,128)(2,1)}, u32[]{:S(2)}) copy-start(bf16[32,2,96,96]{3,2,1,0:T(8,128)(2,1)} %param.18) | copy-start | bytes 3538948
  2.8 1.1 %copy-start.2 = (bf16[32,96,96]{2,1,0:T(8,128)(2,1)S(1)}, bf16[32,96,96]{2,1,0:T(8,128)(2,1)}, u32[]{:S(2)}) copy-start(bf16[32,96,96]{2,1,0:T(8,128)(2,1)} %amps_hbm.1) | copy-start | bytes 1769476
  4.0 0.9 %copy-start.3 = (bf16[2,256,256]{2,1,0:T(8,128)(2,1)S(1)}, bf16[2,256,256]{2,1,0:T(8,128)(2,1)}, u32[]{:S(2)}) copy-start(bf16[2,256,256]{2,1,0:T(8,128)(2,1)} %param.10) | copy-start | bytes 786436
  4.9 0.7 copy-start.4
  5.6 0.7 copy-start.5
  6.3 0.7 copy-start.6
  7.0 0.7 copy-start.7
  7.7 0.7 copy-start.8
  8.3 0.7 copy-start.9

commit v2 on v1

--- a/solution.py
+++ b/solution.py
@@ -24,6 +24,9 @@
 ROWS = 2 * AUX // CHUNKS
 STRIDE = 13
 LANES = 128
+ASK_AT = 2
+PLAN = ((3, 6, 0), (6, 8, 4))
+LAST = 4
 
 
 def dot(a, b, dims):
@@ -36,6 +39,13 @@
     return ((x + sign * dx + 4) % 4 * 4 + (y + sign * dy + 4) % 4) * 2 + (core + dc) % 2
 
 
+def plane_of(device):
+    core, y, x = device % 2, device // 2 % 4, device // 8
+    xs = [(x + d) % 4 * 8 for d in range(4)]
+    ys = [(y + d) % 4 * 2 for d in range(4)]
+    return [xs[k // 8] + ys[k // 2 % 4] + (core + k % 2) % 2 for k in range(PEERS)]
+
+
 def iota(shape, axis):
     return lax.broadcasted_iota(jnp.int32, shape, axis)
 
@@ -55,33 +65,42 @@
 
 
 def kernel(
-    orb_hbm, coeffs_hbm, amps_hbm, inter_hbm, energy, orbitals, nearby, rank, fock, weight,
-    out, orbs, coeffs, amps, masked, inter, first, exchange, coupled, outbox, inbox, asked, table,
-    table_s, asked_s, local_sem, ring_out, ring_in, ask_out, ask_in, amp_out, amp_in,
+    orb_hbm, coeffs_hbm, amps_hbm, inter_hbm, energy_hbm, orbitals_hbm, nearby_hbm, rank_hbm, fock_hbm, weight_hbm,
+    out, orbs, coeffs, amps, masked, inter, energy, orbitals, nearby, rank, fock, weight,
+    first, exchange, coupled, outbox, inbox, asked, table, table_s, asked_s, local_sem, ring_out, ring_in, ask_out, ask_in, amp_out, amp_in,
 ):
     grp = lax.axis_index("grp")
     me = lax.axis_index("pair")
     right = lax.rem(grp + 1, GROUPS)
     left = lax.rem(grp + GROUPS - 1, GROUPS)
 
-    own_orbs = pltpu.make_async_copy(orb_hbm, orbs.at[0], local_sem.at[0])
-    own_coeffs = pltpu.make_async_copy(coeffs_hbm, coeffs, local_sem.at[1])
-    own_amps = pltpu.make_async_copy(amps_hbm, amps, local_sem.at[2])
-    own_inter = pltpu.make_async_copy(inter_hbm, inter, local_sem.at[3])
-    own_orbs.start()
+    def load(i, source, target):
+        copy = pltpu.make_async_copy(source, target, local_sem.at[i])
+        copy.start()
+        return copy
+
+    own_orbs = load(0, orb_hbm, orbs.at[0])
+    own_nearby = load(1, nearby_hbm, nearby)
+    own_orbitals = load(2, orbitals_hbm, orbitals)
+    own_rank = load(3, rank_hbm, rank)
 
     barrier = pltpu.get_barrier_semaphore()
     for target in (right, left):
         pl.semaphore_signal(barrier, inc=1, device_id=(target, me), device_id_type=MESH)
 
-    @pl.loop(1, PEERS)
-    def _(k):
-        pl.semaphore_signal(barrier, inc=1, device_id=(grp, shifted(me, k, 1)), device_id_type=MESH)
-
-    own_amps.start()
-    own_coeffs.start()
-    own_inter.start()
+    plane = plane_of(me)
+    for k in range(1, PEERS):
+        pl.semaphore_signal(barrier, inc=1, device_id=(grp, plane[k]), device_id_type=MESH)
+
+    own_amps = load(4, amps_hbm, amps)
+    own_coeffs = load(5, coeffs_hbm, coeffs)
+    own_inter = load(6, inter_hbm, inter)
+    own_energy = load(7, energy_hbm, energy)
+    own_fock = load(8, fock_hbm, fock)
+    own_weight = load(9, weight_hbm, weight)
     own_orbs.wait()
+    own_nearby.wait()
+    own_orbitals.wait()
     pl.semaphore_wait(barrier, PEERS + 1)
 
     def ring(d, s, c):
@@ -97,7 +116,7 @@
     def ask(k):
         return pltpu.make_async_remote_copy(
             table.at[pl.ds(0, 1)], asked.at[pl.ds(k, 1)], ask_out.at[k], ask_in.at[k],
-            device_id=(grp, shifted(me, k, 1)), device_id_type=MESH,
+            device_id=(grp, plane[k] if isinstance(k, int) else shifted(me, k, 1)), device_id_type=MESH,
         )
 
     def answer(k):
@@ -136,8 +155,7 @@
     pair = iota((PAIRS, 1), 0)
     table[0:1] = (scattered(place[0], wanted[0]) + scattered(place[1], wanted[1])) & (PAIRS - 1)
 
-    @pl.loop(1, PEERS)
-    def _(k):
+    for k in range(1, PEERS):
         ask((k * STRIDE) % PEERS).start()
 
     table[1:2] = (scattered(place[0], 2 * pair) + scattered(place[1], 2 * pair + 1)) & (2 * PAIRS - 1)
@@ -151,9 +169,9 @@
     table[5:6] = scattered(home_place, as_column(second & 1))
     table[6:7] = as_lanes(home_place)
     table[7:8] = as_lanes(as_column(orbitals[0:1] & 1))
-    to_scalar = pltpu.make_async_copy(table, table_s, local_sem.at[4])
-    to_scalar.start()
+    to_scalar = load(10, table, table_s)
     own_amps.wait()
+    own_rank.wait()
 
     def live(p):
         top = rank[p] * (R // 3)
@@ -176,13 +194,20 @@
 
     lax.fori_loop(0, PAIRS, first_pair, 0, unroll=4)
 
+    def forward(s, c):
+        for d in (0, 1):
+            ring(d, s - 1, c).wait_recv()
+            ring(d, s, c).start()
+
+    @pl.loop(0, ASK_AT)
+    def _(c):
+        forward(2, c)
+
     @pl.loop(1, PEERS)
     def _(k):
         ask(k).wait_recv()
 
-    asked_in = pltpu.make_async_copy(asked, asked_s, local_sem.at[5])
-    asked_in.start()
-    asked_in.wait()
+    load(11, asked, asked_s).wait()
 
     @pl.loop(1, PEERS)
     def _(i):
@@ -192,94 +217,105 @@
             outbox[k, j] = jnp.concatenate([blocks[j], blocks[3][:, 32 * j : 32 * j + 32]], axis=1)
         answer(k).start()
 
+    @pl.loop(ASK_AT, CHUNKS)
+    def _(c):
+        forward(2, c)
+
     own_inter.wait()
-
-    def exchange_slot(kz, j):
-        slot = kz * SLOTS + j
-        p, half = table_s[4, slot], table_s[5, slot]
-        block = jnp.where(half == 1, orbs[kz, AUX:], orbs[kz, :AUX])
-        moved = dot(coeffs[p], block, NT).astype(BF16)
-        exchange[slot] = dot(first[p], moved, NT)
-
-    def couple(slot, block):
-        t = inter[table_s[1, slot]]
-        coupled[slot] = dot(dot(t, block, NN).astype(BF16), t, NT)
+    own_energy.wait()
+    own_fock.wait()
+    own_weight.wait()
+
+    def exchange_block(kz):
+        slots = [kz * SLOTS + j for j in range(SLOTS)]
+        pairs = [table_s[4, slot] for slot in slots]
+        halves = [table_s[5, slot] for slot in slots]
+        moved = [
+            dot(coeffs[p], jnp.where(half == 1, orbs[kz, AUX:], orbs[kz, :AUX]), NT).astype(BF16)
+            for p, half in zip(pairs, halves)
+        ]
+        sums = [dot(first[p], m, NT) for p, m in zip(pairs, moved)]
+        for slot, total in zip(slots, sums):
+            exchange[slot] = total
+
+    def couple(slots, blocks):
+        turns = [inter[table_s[1, slot]] for slot in slots]
+        halves = [dot(t, block, NN).astype(BF16) for t, block in zip(turns, blocks)]
+        sums = [dot(half, t, NT) for half, t in zip(halves, turns)]
+        for slot, total in zip(slots, sums):
+            coupled[slot] = total
 
     def couple_own():
-        for j in range(SLOTS):
-            couple(j, masked[table_s[0, j]])
-
-    def couple_peer(k):
-        answer(k).wait_recv()
-        parts = [inbox[k, j] for j in range(3)]
-        for j in range(3):
-            couple(SLOTS * k + j, parts[j][:, :R])
-        couple(SLOTS * k + 3, jnp.concatenate([part[:, R:] for part in parts], axis=1))
-
-    def diagonal(p):
+        couple(range(SLOTS), [masked[table_s[0, j]] for j in range(SLOTS)])
+
+    def couple_peers(begin, n):
+        slots, blocks = [], []
+        for i in range(n):
+            k = ((begin + i) * STRIDE) % PEERS
+            answer(k).wait_recv()
+            parts = [inbox[k, j] for j in range(3)]
+            slots += [SLOTS * k + j for j in range(SLOTS)]
+            blocks += [part[:, :R] for part in parts]
+            blocks.append(jnp.concatenate([part[:, R:] for part in parts], axis=1))
+        if n:
+            couple(slots, blocks)
+
+    def diagonal(p, _):
         across = energy[pl.ds(p, 1), :]
         down = jnp.sum(jnp.where(iota((R, R), 0) == iota((R, R), 1), across, 0.0), axis=1, keepdims=True)
         out[p] = (down + across - (fock[0, p] + fock[1, p])) * amps[p].astype(F32)
-
-    def forward(s, c):
+        return 0
+
+    def exchange_side(s, side):
+        exchange_block(jnp.where(side == 0, s, GROUPS - s))
+
+    done = 1
+    for low, high, n in PLAN:
+        begin = done
+
+        @pl.loop(low, high)
+        def _(s):
+            @pl.loop(0, 2)
+            def _(h):
+                forward(s, 2 * h)
+                exchange_side(s - 2, h)
+                forward(s, 2 * h + 1)
+                couple_peers(begin + (2 * (s - low) + h) * n, n)
+
+        done += (high - low) * 2 * n
+
+        if low == 3:
+            exchange_block(0)
+            couple_own()
+            lax.fori_loop(0, PAIRS, diagonal, 0, unroll=4)
+
+    forward(HALF, 0)
+    forward(HALF, 1)
+    exchange_side(HALF - 2, 0)
+    exchange_side(HALF - 2, 1)
+    couple_peers(done, LAST)
+    done += LAST
+
+    for c in (2, 3):
         for d in (0, 1):
-            ring(d, s - 1, c).wait_recv()
-            ring(d, s, c).start()
-
-    def exchange_some(s, c):
-        kz = jnp.where(c < 2, s, (GROUPS - s) % GROUPS)
-        for j in range(2):
-            exchange_slot(kz, c % 2 * 2 + j)
-
-    @pl.loop(0, CHUNKS)
-    def _(c):
-        forward(2, c)
-        exchange_some(0, c)
-
-        @pl.loop(0, PAIRS // CHUNKS)
-        def _(p):
-            diagonal(c * (PAIRS // CHUNKS) + p)
-
-    couple_own()
-    per_unit = 1
-    begin = 3
-
-    @pl.loop(begin, HALF)
-    def _(s):
-        @pl.loop(0, CHUNKS)
-        def _(c):
-            forward(s, c)
-            exchange_some(s - 2, c)
-            couple_peer((((s - begin) * CHUNKS + c + 1) * STRIDE) % PEERS)
-
-    done = 1 + (HALF - begin) * CHUNKS
+            ring(d, HALF - 1, c).wait_recv()
 
     @pl.loop(0, 2)
-    def _(c):
-        forward(HALF, c)
-        exchange_some(HALF - 2, c)
-
-    @pl.loop(2, CHUNKS)
-    def _(c):
-        ring(0, HALF - 1, c).wait_recv()
-        ring(1, HALF - 1, c).wait_recv()
-        exchange_some(HALF - 2, c)
-
-    @pl.loop(0, CHUNKS)
-    def _(c):
-        exchange_some(HALF - 1, c)
-
-    @pl.loop(done, PEERS)
+    def _(h):
+        exchange_side(HALF - 1, h)
+
+    @pl.loop(0, (PEERS - done) // 2)
     def _(i):
-        couple_peer((i * STRIDE) % PEERS)
+        couple_peers(done + 2 * i, 2)
+
+    couple_peers(done + (PEERS - done) // 2 * 2, (PEERS - done) % 2)
 
     @pl.loop(0, 2)
     def _(c):
         ring(0, HALF, c).wait_recv()
         ring(1, HALF, c).wait_recv()
 
-    for j in range(SLOTS):
-        exchange_slot(HALF, j)
+    exchange_block(HALF)
 
     def finish(p, _):
         near = weight[0, p] * coupled[table_s[2, p]] + weight[1, p] * coupled[table_s[3, p]]
@@ -309,21 +345,24 @@
 def local(
     orbital_ints, pair_fock, pair_orbitals, rank_bucket, pno_coeffs, pno_energy, amplitudes, neighbors, intersections, coupling_fock
 ):
-    far = pl.BlockSpec(memory_space=pltpu.HBM)
-    vector = pl.BlockSpec(memory_space=pltpu.VMEM)
-    scalar = pl.BlockSpec(memory_space=pltpu.SMEM)
     dma = pltpu.SemaphoreType.DMA
     return pl.pallas_call(
         kernel,
         out_shape=jax.ShapeDtypeStruct((PAIRS, R, R), F32),
-        in_specs=[far, far, far, far, vector, vector, vector, scalar, scalar, scalar],
-        out_specs=vector,
+        in_specs=[pl.BlockSpec(memory_space=pltpu.HBM)] * 10,
+        out_specs=pl.BlockSpec(memory_space=pltpu.VMEM),
         scratch_shapes=[
             pltpu.VMEM((GROUPS, 2 * AUX, AUX), BF16),
             pltpu.VMEM((PAIRS, R, AUX), BF16),
             pltpu.VMEM((PAIRS, R, R), BF16),
             pltpu.VMEM((PAIRS, R, R), BF16),
             pltpu.VMEM((2 * PAIRS, R, R), BF16),
+            pltpu.VMEM((PAIRS, R), F32),
+            pltpu.VMEM((2, PAIRS), jnp.int32),
+            pltpu.VMEM((2, PAIRS), jnp.int32),
+            pltpu.SMEM((PAIRS,), jnp.int32),
+            pltpu.SMEM((2, PAIRS), F32),
+            pltpu.SMEM((2, PAIRS), F32),
             pltpu.VMEM((PAIRS, R, AUX), BF16),
             pltpu.VMEM((GROUPS * SLOTS, R, R), F32),
             pltpu.VMEM((PEERS * SLOTS, R, R), F32),
@@ -333,7 +372,7 @@
             pltpu.VMEM((8, LANES), jnp.int32),
             pltpu.SMEM((8, LANES), jnp.int32),
             pltpu.SMEM((PEERS, LANES), jnp.int32),
-            dma((6,)),
+            dma((12,)),
             dma((2, HALF, CHUNKS)),
             dma((2, HALF, CHUNKS)),
             dma((PEERS,)),
@@ -342,7 +381,7 @@
             dma((PEERS,)),
         ],
         compiler_params=pltpu.CompilerParams(
-            collective_id=0, has_side_effects=True, vmem_limit_bytes=48 * 2**20
+            collective_id=0, has_side_effects=True, vmem_limit_bytes=63 * 2**20
         ),
     )(
         orbital_ints.reshape(2 * AUX, AUX),

time: 90.7 us -> 68.3 us (0.75)
  the two profiles are of different devices: /device:TPU:5 before, /device:TPU:8 now
where the time goes in v2:
time: 68.3 us; the launch traced here: 68.2 us
  Pallas kernels  65.5 us (96%)
  local copies, waits for them, and re-layouts  2.66 us (4%)
    pallas_call x1, Pallas kernels, local(): pl.pallas_call(kernel, out_shape=jax.ShapeDtypeStruct((PAIRS, R, R), F32)...  65.5 us
    unnamed x1, local copies, waits for them, and re-layouts  2.66 us

profile of v2, /device:TPU:8, one launch (start us, length us, event | category | flops | bytes accessed | tf_op | source)
XLA Modules:
  0.0 68.2 jit_solution(17696786431631299757)
XLA Ops:
  0.0 65.5 %shard_map.100 = f32[32,96,96]{2,1,0:T(8,128)} custom-call(bf16[512,256]{1,0:T(8,128)(2,1)} %bitcast.9, bf16[32,96,256]{2,1,0:T(8,128)(2,1)} %bitcast.7, bf16[32,96,96]{2,1,0:T(8,128)(2,1)} %amps_hbm.1, bf16[64,96,96]{2,1,0:T(8,128)(2,1)} %bitcast.8, f32[32,96]{1,0:T(8,128)} %energy_hbm.1, s32[2,32]{1,0:T(2,128)} %bitcast.10, s32[2,32]{1,0:T(2,128)} %bitcast.11, ...), custom_call_target="tpu_custom_call" | custom-call | tf_op jit(solution)/shard_map/pallas_call | solution.py:349
  65.5 2.7 %copy.12 = f32[32,96,96]{2,1,0:T(8,128)} copy(f32[32,96,96]{2,1,0:T(8,128)} %shard_map.100) | data formatting | bytes 2359296

commit v3 on v2

--- a/solution.py
+++ b/solution.py
@@ -25,8 +25,8 @@
 STRIDE = 13
 LANES = 128
 ASK_AT = 2
-PLAN = ((3, 6, 0), (6, 8, 4))
-LAST = 4
+PLAN = ((3, 6, 0), (6, 7, 3), (7, 8, 6))
+LAST = 6
 
 
 def dot(a, b, dims):
@@ -345,10 +345,22 @@
 def local(
     orbital_ints, pair_fock, pair_orbitals, rank_bucket, pno_coeffs, pno_energy, amplitudes, neighbors, intersections, coupling_fock
 ):
+    operands = (
+        orbital_ints.reshape(2 * AUX, AUX),
+        jnp.swapaxes(pno_coeffs, 1, 2),
+        amplitudes,
+        intersections.reshape(2 * PAIRS, R, R),
+        pno_energy,
+        pair_orbitals.T,
+        neighbors.T,
+        rank_bucket,
+        pair_fock.T,
+        coupling_fock.T,
+    )
     dma = pltpu.SemaphoreType.DMA
     return pl.pallas_call(
         kernel,
-        out_shape=jax.ShapeDtypeStruct((PAIRS, R, R), F32),
+        out_shape=pltpu.VMEM((PAIRS, R, R), F32),
         in_specs=[pl.BlockSpec(memory_space=pltpu.HBM)] * 10,
         out_specs=pl.BlockSpec(memory_space=pltpu.VMEM),
         scratch_shapes=[
@@ -381,20 +393,9 @@
             dma((PEERS,)),
         ],
         compiler_params=pltpu.CompilerParams(
-            collective_id=0, has_side_effects=True, vmem_limit_bytes=63 * 2**20
+            collective_id=0, has_side_effects=True, vmem_limit_bytes=48 * 2**20
         ),
-    )(
-        orbital_ints.reshape(2 * AUX, AUX),
-        jnp.swapaxes(pno_coeffs, 1, 2),
-        amplitudes,
-        intersections.reshape(2 * PAIRS, R, R),
-        pno_energy,
-        pair_orbitals.T,
-        neighbors.T,
-        rank_bucket,
-        pair_fock.T,
-        coupling_fock.T,
-    )
+    )(*[pltpu.with_memory_space_constraint(operand, pltpu.HBM) for operand in operands])
 
 
 def solution(mesh):

time: 68.3 us -> 64.7 us (0.947)
  Pallas kernels: 65.5 us -> 63.4 us
  local copies, waits for them, and re-layouts: 2.66 us -> 1.15 us
    pallas_call x1, Pallas kernels: 65.5 us -> 63.4 us  [local(): pl.pallas_call(kernel, out_shape=pltpu.VMEM((PAIRS, R, R), F32), in_specs...]
    unnamed x1, local copies, waits for them, and re-layouts: 2.66 us -> 1.15 us
where the time goes in v3:
time: 64.7 us; the launch traced here: 64.6 us
  Pallas kernels  63.4 us (98%)
  local copies, waits for them, and re-layouts  1.15 us (2%)
    pallas_call x1, Pallas kernels, local(): pl.pallas_call(kernel, out_shape=pltpu.VMEM((PAIRS, R, R), F32), in_specs...  63.4 us

profile of v3, /device:TPU:8, one launch (start us, length us, event | category | flops | bytes accessed | tf_op | source)
XLA Modules:
  0.0 64.6 jit_solution(17828646094001310074)
XLA Ops:
  0.0 63.4 %shard_map.100 = f32[32,96,96]{2,1,0:T(8,128)S(1)} custom-call(bf16[512,256]{1,0:T(8,128)(2,1)} %bitcast.9, bf16[32,96,256]{2,1,0:T(8,128)(2,1)} %bitcast.7, bf16[32,96,96]{2,1,0:T(8,128)(2,1)} %amps_hbm.1, bf16[64,96,96]{2,1,0:T(8,128)(2,1)} %bitcast.8, f32[32,96]{1,0:T(8,128)} %energy_hbm.1, s32[2,32]{1,0:T(2,128)} %bitcast.10, s32[2,32]{1,0:T(2,128)} %bitcast.11, ...), custom_call_target="tpu_custom_call" | custom-call | tf_op jit(solution)/shard_map/pallas_call | solution.py:361
  63.4 1.1 %copy.12 = f32[32,96,96]{2,1,0:T(8,128)} copy(f32[32,96,96]{2,1,0:T(8,128)S(1)} %shard_map.100) | data formatting | bytes 2359296

commit v4 on v3

--- a/solution.py
+++ b/solution.py
@@ -192,7 +192,6 @@
         first[p] = dot(coeffs[p], block, NT).astype(BF16)
         return 0
 
-    lax.fori_loop(0, PAIRS, first_pair, 0, unroll=4)
 
     def forward(s, c):
         for d in (0, 1):
@@ -220,6 +219,8 @@
     @pl.loop(ASK_AT, CHUNKS)
     def _(c):
         forward(2, c)
+
+    lax.fori_loop(0, PAIRS, first_pair, 0, unroll=4)
 
     own_inter.wait()
     own_energy.wait()
@@ -310,6 +311,13 @@
 
     couple_peers(done + (PEERS - done) // 2 * 2, (PEERS - done) % 2)
 
+    def settle(p, _):
+        near = weight[0, p] * coupled[table_s[2, p]] + weight[1, p] * coupled[table_s[3, p]]
+        out[p] = out[p] - near
+        return 0
+
+    lax.fori_loop(0, PAIRS, settle, 0, unroll=4)
+
     @pl.loop(0, 2)
     def _(c):
         ring(0, HALF, c).wait_recv()
@@ -318,8 +326,7 @@
     exchange_block(HALF)
 
     def finish(p, _):
-        near = weight[0, p] * coupled[table_s[2, p]] + weight[1, p] * coupled[table_s[3, p]]
-        out[p] = jnp.where(live(p), out[p] + exchange[table_s[6, p]] - near, 0.0)
+        out[p] = jnp.where(live(p), out[p] + exchange[table_s[6, p]], 0.0)
         return 0
 
     lax.fori_loop(0, PAIRS, finish, 0, unroll=4)

time: 64.7 us -> 64.5 us (level)
  no operation moved by 1% of the time
where the time goes in v4:
time: 64.5 us; the launch traced here: 64.4 us
  Pallas kernels  63.2 us (98%)
  local copies, waits for them, and re-layouts  1.15 us (2%)
    pallas_call x1, Pallas kernels, local(): pl.pallas_call(kernel, out_shape=pltpu.VMEM((PAIRS, R, R), F32), in_specs...  63.2 us

profile of v4, /device:TPU:8, one launch (start us, length us, event | category | flops | bytes accessed | tf_op | source)
XLA Modules:
  0.0 64.4 jit_solution(286501168921413154)
XLA Ops:
  0.0 63.2 %shard_map.100 = f32[32,96,96]{2,1,0:T(8,128)S(1)} custom-call(bf16[512,256]{1,0:T(8,128)(2,1)} %bitcast.9, bf16[32,96,256]{2,1,0:T(8,128)(2,1)} %bitcast.7, bf16[32,96,96]{2,1,0:T(8,128)(2,1)} %amps_hbm.1, bf16[64,96,96]{2,1,0:T(8,128)(2,1)} %bitcast.8, f32[32,96]{1,0:T(8,128)} %energy_hbm.1, s32[2,32]{1,0:T(2,128)} %bitcast.10, s32[2,32]{1,0:T(2,128)} %bitcast.11, ...), custom_call_target="tpu_custom_call" | custom-call | tf_op jit(solution)/shard_map/pallas_call | solution.py:368
  63.2 1.1 %copy.12 = f32[32,96,96]{2,1,0:T(8,128)} copy(f32[32,96,96]{2,1,0:T(8,128)S(1)} %shard_map.100) | data formatting | bytes 2359296
